TPU v7x, 128 devices: a whole 4x4x4 slice. The times are simulated.
128 devices in a mesh: row: 16 (over y, x), col: 8 (over z, core).
Axes of the slice: x: 4, y: 4, z: 4, core: 2. Of those that a mesh axis runs over, the one named last changes fastest.
Arguments:
- inputs: bfloat16 [1024, 8192], P('col', 'row'), may hold values from -6 to 6
- out_grad: bfloat16 [1024, 8192], P('col', 'row'), may hold values from -1.5 to 1.5
- gate_pre: bfloat16 [1024, 14336], P('row', 'col'), may hold values from -9 to 9
- up_pre: bfloat16 [1024, 14336], P('row', 'col'), may hold values from -6 to 6
- gate_weight: bfloat16 [8192, 14336], P('row', 'col'), may hold values from -0.0625 to 0.0625
- up_weight: bfloat16 [8192, 14336], P('row', 'col'), may hold values from -0.0625 to 0.0625
- down_weight: bfloat16 [14336, 8192], P('col', 'row'), may hold values from -0.046875 to 0.046875
Outputs:
- input_grad: float32 [1024, 8192], P('col', 'row')
- gate_grad: float32 [8192, 14336], P('row', 'col')
- up_grad: float32 [8192, 14336], P('row', 'col')
- down_grad: float32 [14336, 8192], P('col', 'row')
All inputs are finite; a program needn't handle non-finite values.
Results may differ from a plain program's by a relative error of at most 0.0029.
Values may be sent and summed in bfloat16 or wider, within the bound.
A program may use at most 128 MiB of HBM per device.

v0:
```python
import jax
import jax.numpy as jnp
from jax import lax
from jax.sharding import PartitionSpec as P

LEAD_DIMS = (((0,), (0,)), ((), ()))
LAST_DIMS = (((1,), (1,)), ((), ()))


def swiglu_grads(grad_hidden, gate_pre, up_pre):
    gate_val = gate_pre.astype(jnp.float32)
    up_val = up_pre.astype(jnp.float32)
    gate_sig = jax.nn.sigmoid(gate_val)
    hidden = (gate_val * gate_sig * up_val).astype(jnp.bfloat16)
    grad_gate = (grad_hidden * up_val * gate_sig * (1.0 + gate_val * (1.0 - gate_sig))).astype(
        jnp.bfloat16
    )
    grad_up = (grad_hidden * gate_val * gate_sig).astype(jnp.bfloat16)
    return (hidden, grad_gate, grad_up)


def body(inputs, out_grad, gate_pre, up_pre, gate_weight, up_weight, down_weight):
    input_full, grad_full = (
        lax.all_gather(inputs, "col", axis=0, tiled=True),
        lax.all_gather(out_grad, "col", axis=0, tiled=True),
    )
    partial_sum = lax.dot_general(
        grad_full, down_weight, LAST_DIMS, preferred_element_type=jnp.float32
    )
    grad_hidden = lax.psum(partial_sum, "row")
    gate_all, up_all = (
        lax.all_gather(gate_pre, "row", axis=0, tiled=True),
        lax.all_gather(up_pre, "row", axis=0, tiled=True),
    )
    hidden, grad_gate, grad_up = swiglu_grads(grad_hidden, gate_all, up_all)
    total = lax.dot_general(grad_gate, gate_weight, LAST_DIMS, preferred_element_type=jnp.float32)
    input_grad = lax.psum_scatter(
        total + lax.dot_general(grad_up, up_weight, LAST_DIMS, preferred_element_type=jnp.float32),
        "col",
        scatter_dimension=0,
        tiled=True,
    )
    gate_grad = lax.dot_general(
        input_full, grad_gate, LEAD_DIMS, preferred_element_type=jnp.float32
    )
    up_grad = lax.dot_general(input_full, grad_up, LEAD_DIMS, preferred_element_type=jnp.float32)
    down_grad = lax.dot_general(hidden, grad_full, LEAD_DIMS, preferred_element_type=jnp.float32)
    return (input_grad, gate_grad, up_grad, down_grad)


def solution(mesh):
    in_specs = (
        P("col", "row"),
        P("col", "row"),
        P("row", "col"),
        P("row", "col"),
        P("row", "col"),
        P("row", "col"),
        P("col", "row"),
    )
    out_specs = (P("col", "row"), P("row", "col"), P("row", "col"), P("col", "row"))
    return jax.shard_map(body, mesh=mesh, in_specs=in_specs, out_specs=out_specs, check_vma=False)
```

profile of v0, /device:TPU:0, one launch (start us, length us, event | category | flops | bytes accessed | tf_op | source)
XLA Modules:
  0.0 340.9 jit_solution(9743817639233089111)
XLA Ops:
  7.2 0.0 copy-start
  7.2 0.0 all-gather.5.cloned.1.call-start
  7.2 0.7 all-gather.5.cloned.1.call-update
  7.9 0.0 all-gather.7.cloned.1.call-start
  8.0 0.7 all-gather.7.cloned.1.call-update
  8.7 0.0 all-gather.9.cloned.1.call-start
  8.7 0.7 all-gather.9.cloned.1.call-update
  9.4 0.0 all-reduce.2.cloned.1.call-start
  9.4 26.4 %all-gather.5.cloned.1.call-done = bf16[1024,512]{1,0:T(8,128)(2,1)} async-done(((bf16[128,512]{1,0:T(8,128)(2,1)}), bf16[1024,512]{1,0:T(8,128)(2,1)}) %all-gather.5.cloned.1.call-update) | async-done | bytes 1048592 | tf_op jit(solution)/shard_map/all_gather | solution.py:25
  35.8 0.0 copy-done
  35.8 6.4 %fusion.13 = f32[1024,1792]{1,0:T(8,128)} fusion(bf16[1024,512]{1,0:T(8,128)(2,1)} %all-gather.5.cloned.1.call-done, bf16[1792,512]{1,0:T(8,128)(2,1)S(1)} %copy-done), kind=kOutput, calls=%fused_computation.21 | convolution fusion | flops 1879048192 | bytes 10223616 | tf_op jit(solution)/shard_map/dot_general | solution.py:27
  42.2 0.0 all-reduce.2.cloned.1.call-update
  42.2 0.0 all-gather.11.cloned.1.call-start
  42.2 0.5 all-gather.11.cloned.1.call-update
  42.8 0.0 reduce-scatter.2.cloned.1.call-start
  42.8 44.6 %all-gather.7.cloned.1.call-done = bf16[1024,1792]{1,0:T(8,128)(2,1)} async-done(((bf16[64,1792]{1,0:T(8,128)(2,1)}), bf16[1024,1792]{1,0:T(8,128)(2,1)}) %all-gather.7.cloned.1.call-update) | async-done | bytes 3670032 | tf_op jit(solution)/shard_map/all_gather | solution.py:33
  87.4 50.9 %all-gather.9.cloned.1.call-done = bf16[1024,1792]{1,0:T(8,128)(2,1)} async-done(((bf16[64,1792]{1,0:T(8,128)(2,1)}), bf16[1024,1792]{1,0:T(8,128)(2,1)}) %all-gather.9.cloned.1.call-update) | async-done | bytes 3670032 | tf_op jit(solution)/shard_map/all_gather | solution.py:32
  138.3 133.8 %all-reduce.2.cloned.1.call-done = f32[1024,1792]{1,0:T(8,128)} async-done(((f32[1024,1792]{1,0:T(8,128)}), f32[1024,1792]{1,0:T(8,128)}) %all-reduce.2.cloned.1.call-update) | async-done | bytes 7340048 | tf_op jit(solution)/shard_map/psum | solution.py:30
  272.2 7.1 %fusion.9 = (bf16[1024,1792]{1,0:T(8,128)(2,1)S(1)}, bf16[1024,1792]{1,0:T(8,128)(2,1)S(1)}) fusion(f32[1024,1792]{1,0:T(8,128)} %all-reduce.2.cloned.1.call-done, bf16[1024,1792]{1,0:T(8,128)(2,1)} %all-gather.9.cloned.1.call-done, bf16[1024,1792]{1,0:T(8,128)(2,1)} %all-gather.7.cloned.1.call-done), kind=kLoop, calls=%fused_computation.15 | loop fusion | flops 27525120 | bytes 22020096 | tf_op jit(solution)/shard_map/convert_element_type | solution.py:18
  279.3 0.0 copy-start.2
  279.3 0.0 copy-start.4
  279.4 2.1 fusion.14
  281.5 1.1 copy-done.1
  282.5 3.5 %convolution_add_fusion = f32[1024,512]{1,0:T(8,128)} fusion(f32[1024,512]{1,0:T(8,128)S(1)} %fusion.14, bf16[1024,1792]{1,0:T(8,128)(2,1)S(1)} %get-tuple-element.8, bf16[512,1792]{1,0:T(8,128)(2,1)S(1)} %copy-done.4), kind=kOutput, calls=%fused_computation.19 | convolution fusion | flops 1879572480 | bytes 9699328 | tf_op jit(solution)/shard_map/dot_general | solution.py:38
  286.0 0.0 reduce-scatter.2.cloned.1.call-update
  286.0 7.8 %fusion.10 = f32[1792,512]{1,0:T(8,128)} fusion(bf16[1024,512]{1,0:T(8,128)(2,1)S(1)} %copy-done.5, bf16[1024,1792]{1,0:T(8,128)(2,1)} %all-gather.7.cloned.1.call-done, bf16[1024,1792]{1,0:T(8,128)(2,1)} %all-gather.9.cloned.1.call-done), kind=kOutput, calls=%fused_computation.16 | convolution fusion | flops 1893728256 | bytes 12058624 | tf_op jit(solution)/shard_map/dot_general | solution.py:47
  293.9 3.4 all-gather.11.cloned.1.call-done
  297.3 6.3 %convolution_bitcast_fusion.1 = f32[512,1792]{0,1:T(8,128)} fusion(bf16[1024,1792]{1,0:T(8,128)(2,1)} %copy-done.2, bf16[1024,512]{1,0:T(8,128)(2,1)} %all-gather.11.cloned.1.call-done), kind=kOutput, calls=%fused_computation.18 | convolution fusion | flops 1879048192 | bytes 8388608 | tf_op jit(solution)/shard_map/dot_general | solution.py:43
  303.5 5.2 %copy.11 = f32[512,1792]{1,0:T(8,128)} copy(f32[512,1792]{0,1:T(8,128)} %convolution_bitcast_fusion.1) | data formatting | bytes 7340032
  308.7 6.0 %convolution_bitcast_fusion = f32[512,1792]{0,1:T(8,128)} fusion(bf16[1024,1792]{1,0:T(8,128)(2,1)} %copy-done.1, bf16[1024,512]{1,0:T(8,128)(2,1)S(1)} %copy-done.6), kind=kOutput, calls=%fused_computation.17 | convolution fusion | flops 1879048192 | bytes 8388608 | tf_op jit(solution)/shard_map/dot_general | solution.py:46
  314.7 5.2 %copy.12 = f32[512,1792]{1,0:T(8,128)} copy(f32[512,1792]{0,1:T(8,128)} %convolution_bitcast_fusion) | data formatting | bytes 7340032
  319.9 14.1 %reduce-scatter.2.cloned.1.call-done = f32[128,512]{1,0:T(8,128)} async-done(((f32[1024,512]{1,0:T(8,128)}), f32[128,512]{1,0:T(8,128)}) %reduce-scatter.2.cloned.1.call-update) | async-done | bytes 262160 | tf_op jit(solution)/shard_map/reduce_scatter | solution.py:37
  (9 shorter events, 0.0 us)
Async XLA Ops:
  7.2 28.6 %copy-start = (bf16[1792,512]{1,0:T(8,128)(2,1)S(1)}, bf16[1792,512]{1,0:T(8,128)(2,1)}, u32[]{:S(2)}) copy-start(bf16[1792,512]{1,0:T(8,128)(2,1)} %param.13) | copy-start | bytes 5505028
  7.2 28.6 %all-gather.5.cloned.1.call-start = ((), (), s32[]{:S(2)}) async-start(), calls=%async_computation.1 | async-start | bytes 1179648 | tf_op jit(solution)/shard_map/all_gather | solution.py:25
  7.9 79.5 %all-gather.7.cloned.1.call-start = ((), (), s32[]{:S(2)}) async-start(), calls=%async_computation.3 | async-start | bytes 3899392 | tf_op jit(solution)/shard_map/all_gather | solution.py:33
  8.7 129.7 %all-gather.9.cloned.1.call-start = ((), (), s32[]{:S(2)}) async-start(), calls=%async_computation.4 | async-start | bytes 3899392 | tf_op jit(solution)/shard_map/all_gather | solution.py:32
  9.4 262.8 %all-reduce.2.cloned.1.call-start = ((), (), s32[]{:S(2)}) async-start(), calls=%async_computation.2 | async-start | bytes 14680064 | tf_op jit(solution)/shard_map/psum | solution.py:30
  42.2 255.1 %all-gather.11.cloned.1.call-start = ((), (), s32[]{:S(2)}) async-start(), calls=%async_computation.6 | async-start | bytes 1179648 | tf_op jit(solution)/shard_map/all_gather | solution.py:24
  42.8 291.3 %reduce-scatter.2.cloned.1.call-start = ((), (), s32[]{:S(2)}) async-start(), calls=%async_computation.5 | async-start | bytes 2359296 | tf_op jit(solution)/shard_map/reduce_scatter | solution.py:37
  272.2 7.2 %copy-start.3 = (bf16[512,1792]{1,0:T(8,128)(2,1)S(1)}, bf16[512,1792]{1,0:T(8,128)(2,1)}, u32[]{:S(2)}) copy-start(bf16[512,1792]{1,0:T(8,128)(2,1)} %param.11) | copy-start | bytes 5505028
  279.3 2.1 copy-start.2
  279.3 3.2 copy-start.1
  279.3 3.2 copy-start.4
  282.5 3.5 %copy-start.5 = (bf16[1024,512]{1,0:T(8,128)(2,1)S(1)}, bf16[1024,512]{1,0:T(8,128)(2,1)}, u32[]{:S(2)}) copy-start(bf16[1024,512]{1,0:T(8,128)(2,1)} %all-gather.5.cloned.1.call-done) | copy-start | bytes 3145732
  303.5 5.2 %copy-start.6 = (bf16[1024,512]{1,0:T(8,128)(2,1)S(1)}, bf16[1024,512]{1,0:T(8,128)(2,1)}, u32[]{:S(2)}) copy-start(bf16[1024,512]{1,0:T(8,128)(2,1)} %all-gather.11.cloned.1.call-done) | copy-start | bytes 3145732
Sparse Core Ops, SparseCore 0:
  9.7 26.0 all-gather.4
  37.9 49.4 all-gather.6
  89.5 48.7 all-gather.8
  141.6 130.4 all-reduce.1
  273.8 23.3 all-gather.10
  300.2 33.7 reduce-scatter.1
where the time goes:
time: 341 us
  waiting for transfers between devices  276 us (81%)
  matrix products  32 us (9%)
  between operations  14.2 us (4%)
  local copies, waits for them, and re-layouts  11.4 us (3%)
  other arithmetic  7.15 us (2%)
    psum x1, waiting for transfers between devices, body(): grad_hidden = lax.psum(partial_sum, 'row')  134 us
    all_gather x1, waiting for transfers between devices, body(): lax.all_gather(gate_pre, 'row', axis=0, tiled=True)  50.9 us
    all_gather x1, waiting for transfers between devices, body(): lax.all_gather(up_pre, 'row', axis=0, tiled=True)  44.6 us
    all_gather x1, waiting for transfers between devices, body(): lax.all_gather(out_grad, 'col', axis=0, tiled=True)  26.4 us
    reduce_scatter x1, waiting for transfers between devices, body(): lax.psum_scatter(total + lax.dot_general(grad_up, up_weight, LAST_DIMS, p...  14.1 us
    unnamed x16, local copies, waits for them, and re-layouts  11.4 us
    dot_general x1, matrix products, body(): lax.dot_general(hidden, grad_full, LEAD_DIMS, preferred_element_type=jnp....  7.83 us
    convert_element_type x1, other arithmetic, swiglu_grads(): grad_up = (grad_hidden * gate_val * gate_sig).astype(jnp.bfloat16)  7.15 us
  transfers between devices with their start and end apart: 6, of which 6 were waited for; matrix products, arithmetic and copies ran while one was open for 15% of the time, Pallas kernels for 0%

commit v1 on v0

--- a/solution.py
+++ b/solution.py
@@ -5,6 +5,27 @@
 
 LEAD_DIMS = (((0,), (0,)), ((), ()))
 LAST_DIMS = (((1,), (1,)), ((), ()))
+
+
+def gather_around(shard, axis, dim):
+    count, index, span = (lax.axis_size(axis), lax.axis_index(axis), shard.shape[dim])
+    right = [(i, (i + 1) % count) for i in range(count)]
+    backward = [(i, (i - 1) % count) for i in range(count)]
+    filled = jnp.zeros((*shard.shape[:dim], count * span, *shard.shape[dim + 1 :]), shard.dtype)
+    filled = lax.dynamic_update_slice_in_dim(filled, shard, index * span, axis=dim)
+    from_left = from_right = shard
+    half = count // 2
+    for step in range(1, half + 1):
+        from_left = lax.ppermute(from_left, axis, right)
+        filled = lax.dynamic_update_slice_in_dim(
+            filled, from_left, (index - step) % count * span, axis=dim
+        )
+        if step < count - half:
+            from_right = lax.ppermute(from_right, axis, backward)
+            filled = lax.dynamic_update_slice_in_dim(
+                filled, from_right, (index + step) % count * span, axis=dim
+            )
+    return filled
 
 
 def swiglu_grads(grad_hidden, gate_pre, up_pre):
@@ -22,7 +43,7 @@
 def body(inputs, out_grad, gate_pre, up_pre, gate_weight, up_weight, down_weight):
     input_full, grad_full = (
         lax.all_gather(inputs, "col", axis=0, tiled=True),
-        lax.all_gather(out_grad, "col", axis=0, tiled=True),
+        gather_around(out_grad, "col", 0),
     )
     partial_sum = lax.dot_general(
         grad_full, down_weight, LAST_DIMS, preferred_element_type=jnp.float32

time: 341 us -> 316 us (0.927)
  waiting for transfers between devices: 276 us -> 241 us
  starting transfers between devices: 0.23 us -> 9.92 us
    all_gather x1, waiting for transfers between devices: 50.9 us -> 24.2 us  [body(): lax.all_gather(gate_pre, 'row', axis=0, tiled=True)]
    all_gather x1 -> x0, waiting for transfers between devices: 26.4 us -> none  [body(): lax.all_gather(out_grad, 'col', axis=0, tiled=True)]
    ppermute x0 -> x7, waiting for transfers between devices: none -> 12.6 us  [the longest x4 12.6 us: gather_around(): from_left = lax.ppermute(from_left, axis, right)]
    ppermute x0 -> x7, starting transfers between devices: none -> 9.54 us  [the longest x3 9.51 us: gather_around(): from_right = lax.ppermute(from_right, axis, backward)]
    all_gather x1, waiting for transfers between devices: 44.6 us -> 50.9 us  [body(): lax.all_gather(up_pre, 'row', axis=0, tiled=True)]
    unnamed x16 -> x14, local copies, waits for them, and re-layouts: 11.4 us -> 11.4 us
  transfers between devices with their start and end apart: 6 -> 12, of which waited for: 6 -> 9; matrix products, arithmetic and copies ran while one was open for 15% -> 16% of each run, Pallas kernels for 0% -> 0%
where the time goes in v1:
time: 316 us; the launch traced here: 315 us
  waiting for transfers between devices  241 us (76%)
  matrix products  30.8 us (10%)
  between operations  13.9 us (4%)
  local copies, waits for them, and re-layouts  12.5 us (4%)
  starting transfers between devices  9.92 us (3%)
  other arithmetic  7.15 us (2%)
    psum x1, waiting for transfers between devices, body(): grad_hidden = lax.psum(partial_sum, 'row')  134 us
    all_gather x1, waiting for transfers between devices, body(): lax.all_gather(up_pre, 'row', axis=0, tiled=True)  50.9 us
    all_gather x1, waiting for transfers between devices, body(): lax.all_gather(gate_pre, 'row', axis=0, tiled=True)  24.2 us
    reduce_scatter x1, waiting for transfers between devices, body(): lax.psum_scatter(total + lax.dot_general(grad_up, up_weight, LAST_DIMS, p...  14.1 us
    ppermute x4, waiting for transfers between devices, gather_around(): from_left = lax.ppermute(from_left, axis, right)  12.6 us
    unnamed x14, local copies, waits for them, and re-layouts  11.4 us
    ppermute x3, starting transfers between devices, gather_around(): from_right = lax.ppermute(from_right, axis, backward)  9.51 us
    dot_general x1, matrix products, body(): lax.dot_general(hidden, grad_full, LEAD_DIMS, preferred_element_type=jnp....  7.82 us
  transfers between devices with their start and end apart: 12, of which 9 were waited for; matrix products, arithmetic and copies ran while one was open for 16% of the time, Pallas kernels for 0%

profile of v1, /device:TPU:0, one launch (start us, length us, event | category | flops | bytes accessed | tf_op | source)
XLA Modules:
  0.0 315.5 jit_solution(10186230406202325329)
XLA Ops:
  7.2 0.0 all-gather.6.cloned.1.call-start
  7.2 0.7 all-gather.6.cloned.1.call-update
  7.9 0.0 all-gather.4.cloned.1.call-start
  8.0 0.7 all-gather.4.cloned.1.call-update
  8.7 0.0 all-reduce.2.cloned.1.call-start
  8.7 3.6 %collective-permute-start.1 = (bf16[128,512]{1,0:T(8,128)(2,1)}, bf16[128,512]{1,0:T(8,128)(2,1)S(1)}, u32[]{:S(2)}, u32[]{:S(2)}) collective-permute-start(bf16[128,512]{1,0:T(8,128)(2,1)} %param.8), channel_id=1, source_target_pairs={{0,7},{1,0},{2,1},{3,2},{4,3},{5,4},{6,5},{7,6},{8,15},{9,8},{10,9... | collective-permute-start | bytes 393224 | tf_op jit(solution)/shard_map/ppermute | solution.py:24
  12.3 0.1 broadcast_in_dim.3
  12.4 0.9 constant_dynamic-update-slice_fusion.7
  13.3 1.8 collective-permute-done
  15.2 3.0 collective-permute-start.3
  18.2 2.6 collective-permute-done.2
  20.8 3.0 collective-permute-start.5
  23.8 2.6 collective-permute-done.4
  26.4 5.5 %collective-permute-done.6 = bf16[128,512]{1,0:T(8,128)(2,1)S(1)} collective-permute-done((bf16[128,512]{1,0:T(8,128)(2,1)S(1)}, bf16[128,512]{1,0:T(8,128)(2,1)S(1)}, u32[]{:S(2)}, u32[]{:S(2)}) %collective-permute-start.6) | collective-permute-done | bytes 131104 | tf_op jit(solution)/shard_map/ppermute | solution.py:19
  32.0 5.1 %fusion.13 = f32[1024,1792]{1,0:T(8,128)} fusion(bf16[1024,512]{1,0:T(8,128)(2,1)S(1)} %constant_dynamic-update-slice_fusion, bf16[1792,512]{1,0:T(8,128)(2,1)S(1)} %copy-done), kind=kOutput, calls=%fused_computation.29 | convolution fusion | flops 1879048192 | bytes 10223616 | tf_op jit(solution)/shard_map/dot_general | solution.py:48
  37.1 0.0 all-gather.8.cloned.1.call-start
  37.2 0.5 all-gather.8.cloned.1.call-update
  37.7 0.2 reduce-scatter.2.cloned.1.call-start
  38.0 24.2 %all-gather.6.cloned.1.call-done = bf16[1024,1792]{1,0:T(8,128)(2,1)} async-done(((bf16[64,1792]{1,0:T(8,128)(2,1)}), bf16[1024,1792]{1,0:T(8,128)(2,1)}) %all-gather.6.cloned.1.call-update) | async-done | bytes 3670032 | tf_op jit(solution)/shard_map/all_gather | solution.py:53
  62.2 50.9 %all-gather.4.cloned.1.call-done = bf16[1024,1792]{1,0:T(8,128)(2,1)} async-done(((bf16[64,1792]{1,0:T(8,128)(2,1)}), bf16[1024,1792]{1,0:T(8,128)(2,1)}) %all-gather.4.cloned.1.call-update) | async-done | bytes 3670032 | tf_op jit(solution)/shard_map/all_gather | solution.py:54
  113.1 134.0 %all-reduce.2.cloned.1.call-done = f32[1024,1792]{1,0:T(8,128)} async-done(((f32[1024,1792]{1,0:T(8,128)}), f32[1024,1792]{1,0:T(8,128)}) %all-reduce.2.cloned.1.call-update) | async-done | bytes 7340048 | tf_op jit(solution)/shard_map/psum | solution.py:51
  247.1 7.1 %fusion.9 = (bf16[1024,1792]{1,0:T(8,128)(2,1)S(1)}, bf16[1024,1792]{1,0:T(8,128)(2,1)S(1)}) fusion(f32[1024,1792]{1,0:T(8,128)} %all-reduce.2.cloned.1.call-done, bf16[1024,1792]{1,0:T(8,128)(2,1)} %all-gather.6.cloned.1.call-done, bf16[1024,1792]{1,0:T(8,128)(2,1)} %all-gather.4.cloned.1.call-done), kind=kLoop, calls=%fused_computation.15 | loop fusion | flops 27525120 | bytes 22020096 | tf_op jit(solution)/shard_map/convert_element_type | solution.py:39
  254.3 2.1 fusion.14
  256.4 1.1 copy-done.1
  257.5 3.5 %convolution_add_fusion = f32[1024,512]{1,0:T(8,128)} fusion(f32[1024,512]{1,0:T(8,128)S(1)} %fusion.14, bf16[1024,1792]{1,0:T(8,128)(2,1)S(1)} %get-tuple-element.8, bf16[512,1792]{1,0:T(8,128)(2,1)S(1)} %copy-done.4), kind=kOutput, calls=%fused_computation.19 | convolution fusion | flops 1879572480 | bytes 9699328 | tf_op jit(solution)/shard_map/dot_general | solution.py:59
  261.0 7.8 %fusion.10 = f32[1792,512]{1,0:T(8,128)} fusion(bf16[1024,512]{1,0:T(8,128)(2,1)S(1)} %constant_dynamic-update-slice_fusion, bf16[1024,1792]{1,0:T(8,128)(2,1)} %all-gather.4.cloned.1.call-done, bf16[1024,1792]{1,0:T(8,128)(2,1)} %all-gather.6.cloned.1.call-done), kind=kOutput, calls=%fused_computation.16 | convolution fusion | flops 1893728256 | bytes 12058624 | tf_op jit(solution)/shard_map/dot_general | solution.py:68
  268.8 3.4 %all-gather.8.cloned.1.call-done = bf16[1024,512]{1,0:T(8,128)(2,1)} async-done(((bf16[128,512]{1,0:T(8,128)(2,1)}), bf16[1024,512]{1,0:T(8,128)(2,1)}) %all-gather.8.cloned.1.call-update) | async-done | bytes 1048592 | tf_op jit(solution)/shard_map/all_gather | solution.py:45
  272.2 6.3 %convolution_bitcast_fusion.1 = f32[512,1792]{0,1:T(8,128)} fusion(bf16[1024,1792]{1,0:T(8,128)(2,1)} %copy-done.2, bf16[1024,512]{1,0:T(8,128)(2,1)} %all-gather.8.cloned.1.call-done), kind=kOutput, calls=%fused_computation.18 | convolution fusion | flops 1879048192 | bytes 8388608 | tf_op jit(solution)/shard_map/dot_general | solution.py:64
  278.5 5.2 %copy.11 = f32[512,1792]{1,0:T(8,128)} copy(f32[512,1792]{0,1:T(8,128)} %convolution_bitcast_fusion.1) | data formatting | bytes 7340032
  283.7 6.0 %convolution_bitcast_fusion = f32[512,1792]{0,1:T(8,128)} fusion(bf16[1024,1792]{1,0:T(8,128)(2,1)} %copy-done.1, bf16[1024,512]{1,0:T(8,128)(2,1)S(1)} %copy-done.5), kind=kOutput, calls=%fused_computation.17 | convolution fusion | flops 1879048192 | bytes 8388608 | tf_op jit(solution)/shard_map/dot_general | solution.py:67
  289.7 5.1 %copy.12 = f32[512,1792]{1,0:T(8,128)} copy(f32[512,1792]{0,1:T(8,128)} %convolution_bitcast_fusion) | data formatting | bytes 7340032
  294.9 14.1 %reduce-scatter.2.cloned.1.call-done = f32[128,512]{1,0:T(8,128)} async-done(((f32[1024,512]{1,0:T(8,128)}), f32[128,512]{1,0:T(8,128)}) %reduce-scatter.2.cloned.1.call-update) | async-done | bytes 262160 | tf_op jit(solution)/shard_map/reduce_scatter | solution.py:58
  (27 shorter events, 0.2 us)
Async XLA Ops:
  7.2 24.8 %copy-start = (bf16[1792,512]{1,0:T(8,128)(2,1)S(1)}, bf16[1792,512]{1,0:T(8,128)(2,1)}, u32[]{:S(2)}) copy-start(bf16[1792,512]{1,0:T(8,128)(2,1)} %param.13) | copy-start | bytes 5505028
  7.2 55.0 %all-gather.6.cloned.1.call-start = ((), (), s32[]{:S(2)}) async-start(), calls=%async_computation.3 | async-start | bytes 3899392 | tf_op jit(solution)/shard_map/all_gather | solution.py:53
  7.9 105.2 %all-gather.4.cloned.1.call-start = ((), (), s32[]{:S(2)}) async-start(), calls=%async_computation.2 | async-start | bytes 3899392 | tf_op jit(solution)/shard_map/all_gather | solution.py:54
  8.7 238.5 %all-reduce.2.cloned.1.call-start = ((), (), s32[]{:S(2)}) async-start(), calls=%async_computation.1 | async-start | bytes 14680064 | tf_op jit(solution)/shard_map/psum | solution.py:51
  8.7 6.4 %collective-permute-start = (bf16[128,512]{1,0:T(8,128)(2,1)}, bf16[128,512]{1,0:T(8,128)(2,1)S(1)}, u32[]{:S(2)}, u32[]{:S(2)}) collective-permute-start(bf16[128,512]{1,0:T(8,128)(2,1)} %param.8), channel_id=1, source_target_pairs={{0,1},{1,2},{2,3},{3,4},{4,5},{5,6},{6,7},{7,0},{8,9},{9,10},{10,1... | collective-permute-start | bytes 393224 | tf_op jit(solution)/shard_map/ppermute | solution.py:19
  8.7 6.4 %collective-permute-start.1 = (bf16[128,512]{1,0:T(8,128)(2,1)}, bf16[128,512]{1,0:T(8,128)(2,1)S(1)}, u32[]{:S(2)}, u32[]{:S(2)}) collective-permute-start(bf16[128,512]{1,0:T(8,128)(2,1)} %param.8), channel_id=1, source_target_pairs={{0,7},{1,0},{2,1},{3,2},{4,3},{5,4},{6,5},{7,6},{8,15},{9,8},{10,9... | collective-permute-start | bytes 393224 | tf_op jit(solution)/shard_map/ppermute | solution.py:24
  15.1 5.6 %collective-permute-start.2 = (bf16[128,512]{1,0:T(8,128)(2,1)S(1)}, bf16[128,512]{1,0:T(8,128)(2,1)S(1)}, u32[]{:S(2)}, u32[]{:S(2)}) collective-permute-start(bf16[128,512]{1,0:T(8,128)(2,1)S(1)} %collective-permute-done), channel_id=1, source_target_pairs={{0,1},{1,2},{2,3},{3,4},{4,5},{5,6},{6,7},{7,0},{8,9},{9,10},{10,1... | collective-permute-start | bytes 393224 | tf_op jit(solution)/shard_map/ppermute | solution.py:19
  15.2 5.6 %collective-permute-start.3 = (bf16[128,512]{1,0:T(8,128)(2,1)S(1)}, bf16[128,512]{1,0:T(8,128)(2,1)S(1)}, u32[]{:S(2)}, u32[]{:S(2)}) collective-permute-start(bf16[128,512]{1,0:T(8,128)(2,1)S(1)} %collective-permute-done.1), channel_id=1, source_target_pairs={{0,7},{1,0},{2,1},{3,2},{4,3},{5,4},{6,5},{7,6},{8,15},{9,8},{10,9... | collective-permute-start | bytes 393224 | tf_op jit(solution)/shard_map/ppermute | solution.py:24
  20.8 5.6 %collective-permute-start.4 = (bf16[128,512]{1,0:T(8,128)(2,1)S(1)}, bf16[128,512]{1,0:T(8,128)(2,1)S(1)}, u32[]{:S(2)}, u32[]{:S(2)}) collective-permute-start(bf16[128,512]{1,0:T(8,128)(2,1)S(1)} %collective-permute-done.2), channel_id=1, source_target_pairs={{0,1},{1,2},{2,3},{3,4},{4,5},{5,6},{6,7},{7,0},{8,9},{9,10},{10,1... | collective-permute-start | bytes 393224 | tf_op jit(solution)/shard_map/ppermute | solution.py:19
  20.8 5.6 %collective-permute-start.5 = (bf16[128,512]{1,0:T(8,128)(2,1)S(1)}, bf16[128,512]{1,0:T(8,128)(2,1)S(1)}, u32[]{:S(2)}, u32[]{:S(2)}) collective-permute-start(bf16[128,512]{1,0:T(8,128)(2,1)S(1)} %collective-permute-done.3), channel_id=1, source_target_pairs={{0,7},{1,0},{2,1},{3,2},{4,3},{5,4},{6,5},{7,6},{8,15},{9,8},{10,9... | collective-permute-start | bytes 393224 | tf_op jit(solution)/shard_map/ppermute | solution.py:24
  26.4 5.6 %collective-permute-start.6 = (bf16[128,512]{1,0:T(8,128)(2,1)S(1)}, bf16[128,512]{1,0:T(8,128)(2,1)S(1)}, u32[]{:S(2)}, u32[]{:S(2)}) collective-permute-start(bf16[128,512]{1,0:T(8,128)(2,1)S(1)} %collective-permute-done.4), channel_id=1, source_target_pairs={{0,1},{1,2},{2,3},{3,4},{4,5},{5,6},{6,7},{7,0},{8,9},{9,10},{10,1... | collective-permute-start | bytes 393224 | tf_op jit(solution)/shard_map/ppermute | solution.py:19
  37.1 235.1 %all-gather.8.cloned.1.call-start = ((), (), s32[]{:S(2)}) async-start(), calls=%async_computation.5 | async-start | bytes 1179648 | tf_op jit(solution)/shard_map/all_gather | solution.py:45
  37.7 271.2 %reduce-scatter.2.cloned.1.call-start = ((), (), s32[]{:S(2)}) async-start(), calls=%async_computation.4 | async-start | bytes 2359296 | tf_op jit(solution)/shard_map/reduce_scatter | solution.py:58
  247.1 7.2 %copy-start.3 = (bf16[512,1792]{1,0:T(8,128)(2,1)S(1)}, bf16[512,1792]{1,0:T(8,128)(2,1)}, u32[]{:S(2)}) copy-start(bf16[512,1792]{1,0:T(8,128)(2,1)} %param.11) | copy-start | bytes 5505028
  254.3 2.1 copy-start.2
  254.3 3.2 %copy-start.1 = (bf16[1024,1792]{1,0:T(8,128)(2,1)}, bf16[1024,1792]{1,0:T(8,128)(2,1)S(1)}, u32[]{:S(2)}) copy-start(bf16[1024,1792]{1,0:T(8,128)(2,1)S(1)} %get-tuple-element.8) | copy-start | bytes 11010052
  254.3 3.2 %copy-start.4 = (bf16[512,1792]{1,0:T(8,128)(2,1)S(1)}, bf16[512,1792]{1,0:T(8,128)(2,1)}, u32[]{:S(2)}) copy-start(bf16[512,1792]{1,0:T(8,128)(2,1)} %param.12) | copy-start | bytes 5505028
  278.5 5.2 %copy-start.5 = (bf16[1024,512]{1,0:T(8,128)(2,1)S(1)}, bf16[1024,512]{1,0:T(8,128)(2,1)}, u32[]{:S(2)}) copy-start(bf16[1024,512]{1,0:T(8,128)(2,1)} %all-gather.8.cloned.1.call-done) | copy-start | bytes 3145732
Sparse Core Ops, SparseCore 0:
  10.1 51.9 all-gather.5
  64.3 48.7 all-gather.3
  116.6 130.5 all-reduce.1
  248.8 23.3 all-gather.7
  275.2 33.7 reduce-scatter.1
